TPU v7x, 32 devices: a whole 2x2x4 slice. The times are simulated.
32 devices in a mesh: site: 2 (over x), gx: 16 (over z, y, core).
Axes of the slice: x: 2, y: 2, z: 4, core: 2. Of those that a mesh axis runs over, the one named last changes fastest.
Arguments:
- velocity: float32 [3, 256, 32, 128], P(None, ('site', 'gx')), parts along dimension 1, may hold values from -6 to 6
- stress: float32 [6, 256, 32, 128], P(None, ('site', 'gx')), parts along dimension 1, may hold values from -6 to 6
- material: int32 [128, 32, 128], P('gx'), may hold values from 0 to 7
- buoyancy_table: float32 [8], replicated, may hold values from 0.7 to 1.4
- lame_table: float32 [8], replicated, may hold values from 0.1 to 0.3
- shear_table: float32 [8], replicated, may hold values from 0.1 to 0.35
- fault_cells: int32 [64, 128], P('gx'), may hold values from 0 to 32767
- block_count: int32 [16], P('gx'), may hold values from 1 to 4, as said below
- strain_history: bfloat16 [128, 6, 128, 512], P(('site', 'gx')), parts along dimension 0, may hold values from -6 to 6
- slip_weights: bfloat16 [64, 256, 768], P('gx'), may hold values from -0.0390625 to 0.0390625
Outputs:
- velocity_out: float32 [3, 256, 32, 128], P(None, ('site', 'gx')), parts along dimension 1
- stress_out: float32 [6, 256, 32, 128], P(None, ('site', 'gx')), parts along dimension 1
- seismograms: float32 [512, 512], P(('site', 'gx')), parts along dimension 0
There are 2 independent parts, one for each index of `site`. A program takes and returns all parts, laid end to end along the dimension named above; an argument that names none is the same for every part. Nothing has to cross between parts.
Inputs may be any that keep to these rules, and one draw needn't show every extreme that they name: `block_count`: live blocks of a device are its first slots; some device has 4 of them. `fault_cells`: cells are numbered row-major over one device's 8 x 32 x 128 slab.
All inputs are finite; a program needn't handle non-finite values.
Results may differ from a plain program's by a relative error of at most 0.00049.
Values may be sent and summed in bfloat16 or wider, within the bound.
No kernel may reach another device: no remote copies, remote signals or barrier semaphores. Data moves between devices by JAX's collectives and lax.ppermute only.
A program may use at most 128 MiB of HBM per device.

v0:
```python
import functools

import jax
import jax.numpy as jnp
from jax import lax
from jax.experimental import pallas as pl
from jax.experimental.pallas import tpu as pltpu
from jax.sharding import PartitionSpec as P

time_step = 0.4
scale = time_step / 24.0

VX, VY, VZ, SXX, SYY, SZZ, SXY, SXZ, SYZ, MAT = range(10)
LOWER_RAW = (2, 1, 1, 3, 1, 1, 3, 3, 1, 3)
UPPER_RAW = (1, 2, 2, 3, 2, 2, 3, 3, 2, 3)
LOWER_MOVED = ((3, 5), (2, 4), (2, 4))
UPPER_MOVED = ((2, 4), (3, 5), (3, 5))
LOWER_FINE = (VX, VY, VZ, SXX, SXY, SXZ, SYZ)
UPPER_FINE = (VY, VZ, SXX)
RAW, MOVED, FINE = range(3)
EDGE = 5
RIM = 8


def halo_list(raw, moved, fine):
    entries = [(RAW, field, depth) for field in range(10) for depth in range(1, raw[field] + 1)]
    for field, (first, last) in enumerate(moved):
        entries += [(MOVED, field, depth) for depth in range(first, last + 1)]
    return entries + [(FINE, field, 1) for field in fine]


LOWER = halo_list(LOWER_RAW, LOWER_MOVED, LOWER_FINE)
UPPER = halo_list(UPPER_RAW, UPPER_MOVED, UPPER_FINE)
HALO = max(len(LOWER), len(UPPER))

f32 = jnp.float32
bf16 = jnp.bfloat16


def second_core():
    return lax.axis_index("gx") % 2


def fetch_all(sources, targets, sems):
    copies = [
        pltpu.make_async_copy(source, target, sems.at[index])
        for index, (source, target) in enumerate(zip(sources, targets))
    ]
    for copy in copies:
        copy.start()
    return copies


def looked_up(code, tables):
    results = [jnp.zeros(code.shape, f32) for _ in tables]
    for entry in range(len(tables[0])):
        hit = code == entry + 1
        results = [jnp.where(hit, table[entry], result) for table, result in zip(tables, results)]
    return results


def parts_of(behind, here_low, here_high, ahead):
    return here_high - here_low, ahead - behind


def joined(*parts):
    near, far = parts[0]
    for more_near, more_far in parts[1:]:
        near, far = near + more_near, far + more_far
    return 27.0 * near - far


def shifted(values, place, axis, by):
    size = values.shape[axis]
    inside = place < size - by if by > 0 else place >= -by
    return jnp.where(inside, pltpu.roll(values, -by % size, axis), 0.0)


def along(values, place, axis, forward):
    offsets = (-1, 0, 1, 2) if forward else (-2, -1, 0, 1)
    return parts_of(*[values if by == 0 else shifted(values, place, axis, by) for by in offsets])


def stepping(moving, pulling, rows, lanes):
    inner = pl.ds(RIM, rows)
    lane = lax.broadcasted_iota(jnp.int32, (rows, lanes), 1)

    def store(field, place, values):
        if field < 3:
            moving[field, place, inner] = values
        else:
            pulling[field - 3, place, inner] = values

    def read(field, place, at=inner):
        return moving[field, place, at] if field < 3 else pulling[field - 3, place, at]

    def along_x(field, place, forward):
        start = place - 1 if forward else place - 2
        return parts_of(*[read(field, start + step) for step in range(4)])

    def along_y(field, place, forward):
        start = RIM - 1 if forward else RIM - 2
        return parts_of(*[read(field, place, pl.ds(start + step, rows)) for step in range(4)])

    def along_z(field, place, forward):
        return along(read(field, place), lane, 1, forward)

    def pull(field, place):
        if field == VX:
            return joined(along_x(SXX, place, True), along_y(SXY, place, False), along_z(SXZ, place, False))
        if field == VY:
            return joined(along_x(SXY, place, False), along_y(SYY, place, True), along_z(SYZ, place, False))
        return joined(along_x(SXZ, place, False), along_y(SYZ, place, False), along_z(SZZ, place, True))

    return store, read, along_x, along_y, along_z, pull


def pack_kernel(
    velocity_from,
    stress_from,
    material_from,
    buoyancy_from,
    across,
    within,
    moving,
    pulling,
    material,
    buoyancy,
    sems,
):
    planes, rows, lanes = material.shape
    slab, inner = pl.ds(EDGE, planes), pl.ds(RIM, rows)
    copies = fetch_all(
        (stress_from, velocity_from, material_from, buoyancy_from),
        (pulling.at[:, slab, inner], moving.at[:, slab, inner], material, buoyancy),
        sems,
    )
    blank = jnp.zeros((moving.shape[1], RIM, lanes), f32)
    for ref, fields_along_y in ((moving, (0, 1, 2)), (pulling, (SXY - 3, SYY - 3, SYZ - 3))):
        for field in fields_along_y:
            ref[field, :, 0:RIM] = blank
            ref[field, :, RIM + rows : 2 * RIM + rows] = blank
    store, read, along_x, along_y, along_z, pull = stepping(moving, pulling, rows, lanes)
    odd = second_core()
    for copy in copies:
        copy.wait()

    def moved(field, plane):
        entries = [buoyancy[entry] for entry in range(buoyancy.shape[0])]
        factor = scale * looked_up(material[plane] + 1, (entries,))[0]
        return read(field, EDGE + plane) + factor * pull(field, EDGE + plane)

    def fill(out, entries, plane_of):
        for index, (what, field, depth) in enumerate(entries):
            plane = plane_of(depth)
            if what == MOVED:
                values = moved(field, plane)
            elif field < 9:
                values = read(field, EDGE + plane)
            else:
                values = (material[plane] + 1).astype(f32)
            if what == FINE:
                values = values - values.astype(bf16).astype(f32)
            out[index] = values.astype(bf16)
        for spare in range(len(entries), out.shape[0]):
            out[spare] = jnp.zeros(out.shape[1:], bf16)

    def upper_face(out):
        fill(out, LOWER, lambda depth: planes - depth)

    def lower_face(out):
        fill(out, UPPER, lambda depth: depth - 1)

    @pl.when(odd == 0)
    def _():
        lower_face(across)
        upper_face(within)

    @pl.when(odd != 0)
    def _():
        upper_face(across)
        lower_face(within)


def in_steps(values):
    largest = jnp.max(jnp.abs(values), axis=1, keepdims=True)
    exponent = jnp.ceil(jnp.log2(jnp.maximum(largest, 1e-30))) - 14.0
    return exponent, jnp.clip(jnp.round(values * jnp.exp2(-exponent)), -32767.0, 32767.0)


def history_kernel(live, weights, history, after, kept, sent, slips, records, total, slip_sems, record_sems):
    del after
    slots = weights.shape[0]
    copies = [
        (
            pltpu.make_async_copy(weights.at[slot], slips.at[slot], slip_sems.at[slot]),
            pltpu.make_async_copy(history.at[slot], records.at[slot], record_sems.at[slot]),
        )
        for slot in range(slots)
    ]
    for copy in copies[0]:
        copy.start()
    for slot in range(1, slots):

        @pl.when(slot < live[0])
        def _(slot=slot):
            for copy in copies[slot]:
                copy.start()

    for copy in copies[0]:
        copy.wait()
    total[...] = jnp.dot(slips[0], records[0], preferred_element_type=f32)
    for slot in range(1, slots):

        @pl.when(slot < live[0])
        def _(slot=slot):
            for copy in copies[slot]:
                copy.wait()
            total[...] += jnp.dot(slips[slot], records[slot], preferred_element_type=f32)

    half = kept.shape[1]
    first = second_core() == 0
    early, late = total[:, :half], total[:, half:]
    early = jnp.where(lax.broadcasted_iota(jnp.int32, early.shape, 1) < 2, 0.0, early)
    kept[...] = jnp.where(first, early, late)
    sent[...] = jnp.where(first, late, early)


def ready_kernel(
    kept,
    received,
    velocity_from,
    stress_from,
    material_from,
    buoyancy_from,
    lame_from,
    shear_from,
    partial,
    exponents,
    velocity,
    stress,
    material,
    entries,
    buoyancy,
    lame,
    shear,
    sems,
):
    copies = fetch_all(
        (buoyancy_from, lame_from, shear_from, stress_from, velocity_from, material_from),
        (buoyancy, lame, shear, stress, velocity, material),
        sems,
    )
    exponent, steps = in_steps(kept[...] + received[...])
    partial[...] = steps.astype(jnp.int32).astype(jnp.int16)
    exponents[...] = jnp.broadcast_to(exponent, exponents.shape)
    for copy in copies[:3]:
        copy.wait()
    for kind, table in enumerate((buoyancy, lame, shear)):
        for entry in range(table.shape[0]):
            at = kind * table.shape[0] + entry
            entries[at : at + 1] = jnp.full((1, entries.shape[1]), table[entry], f32)
    for copy in copies[3:]:
        copy.wait()


def steps_kernel(
    live,
    cells_from,
    weights,
    velocity,
    stress,
    material,
    entries,
    across,
    within,
    partial,
    exponents,
    velocity_out,
    stress_out,
    sums,
    moving,
    pulling,
    factors,
    strain_factors,
    strains,
    early,
    slips,
    cells,
    tail,
    cell_sem,
    slip_sem,
    out_sems,
):
    planes, rows, lanes = material.shape
    materials = entries.shape[0] // 3
    tables = [
        [entries[at : at + 1] for at in range(kind * materials, (kind + 1) * materials)] for kind in range(3)
    ]
    inner = pl.ds(RIM, rows)
    slab = pl.ds(EDGE, planes)
    cell_copy = pltpu.make_async_copy(cells_from, cells, cell_sem)
    cell_copy.start()
    slip_copy = pltpu.make_async_copy(weights, slips, slip_sem)
    slip_copy.start()
    half = partial.shape[1]
    sum_copies = [
        pltpu.make_async_copy(partial, sums.at[:, pl.ds(0, half)], out_sems.at[2]),
        pltpu.make_async_copy(tail, sums.at[:, pl.ds(half, lanes)], out_sems.at[3]),
    ]
    sum_copies[0].start()
    odd = second_core()
    store, read, along_x, along_y, along_z, pull = stepping(moving, pulling, rows, lanes)

    blank = jnp.zeros((moving.shape[1], RIM, lanes), f32)
    for ref, fields_along_y in ((moving, (0, 1, 2)), (pulling, (SXY - 3, SYY - 3, SYZ - 3))):
        for field in fields_along_y:
            ref[field, :, 0:RIM] = blank
            ref[field, :, RIM + rows : 2 * RIM + rows] = blank
    moving[:, slab, inner] = velocity[...]
    pulling[:, slab, inner] = stress[...]

    for plane in range(planes):
        buoyancy, lame, shear = looked_up(material[plane] + 1, tables)
        factors[0, EDGE + plane] = scale * buoyancy
        factors[1, EDGE + plane] = scale * lame
        factors[2, EDGE + plane] = scale * shear
        strain_factors[0, plane] = lame / (3.0 * lame + 2.0 * shear)
        strain_factors[1, plane] = 1.0 / (2.0 * shear)

    def unpack(halo, upper):
        entries = UPPER if upper else LOWER
        for index, (what, field, depth) in enumerate(entries):
            if what == FINE:
                continue
            place = EDGE + planes + depth - 1 if upper else EDGE - depth
            values = halo[index].astype(f32)
            if what == RAW and (FINE, field, depth) in entries:
                values = values + halo[entries.index((FINE, field, depth))].astype(f32)
            if field < 9:
                store(field, place, values)
            else:
                found = looked_up(values.astype(jnp.int32), tables)
                for kind in range(3):
                    factors[kind, place] = scale * found[kind]

    @pl.when(odd == 0)
    def _():
        unpack(across, False)
        unpack(within, True)

    @pl.when(odd != 0)
    def _():
        unpack(within, False)
        unpack(across, True)

    def move(place, do_x=True, do_yz=True):
        buoyancy = factors[0, place]
        chosen = ([VX] if do_x else []) + ([VY, VZ] if do_yz else [])
        results = [read(field, place) + buoyancy * pull(field, place) for field in chosen]
        for field, values in zip(chosen, results):
            store(field, place, values)

    def strain(place, do_yz=True, keep=None):
        lame, shear = factors[1, place], factors[2, place]
        twice = 2.0 * shear
        exx = joined(along_x(VX, place, False))
        eyy = joined(along_y(VY, place, False))
        ezz = joined(along_z(VZ, place, False))
        common = lame * (exx + eyy + ezz)
        changes = [(SXX, common + twice * exx)]
        changes.append((SXY, shear * joined(along_y(VX, place, True), along_x(VY, place, True))))
        changes.append((SXZ, shear * joined(along_z(VX, place, True), along_x(VZ, place, True))))
        if do_yz:
            changes.append((SYY, common + twice * eyy))
            changes.append((SZZ, common + twice * ezz))
            changes.append((SYZ, shear * joined(along_z(VY, place, True), along_y(VZ, place, True))))
        results = {field: read(field, place) + change for field, change in changes}
        for field, values in results.items():
            store(field, place, values)
        if keep is not None:
            compliance = strain_factors[1, place - EDGE]
            shift = strain_factors[0, place - EDGE] * (results[SXX] + results[SYY] + results[SZZ])
            first = pl.multiple_of((place - EDGE) * (8 * rows), 8 * rows)
            for field in range(3, 9):
                values = results[field] - shift if field < 6 else results[field]
                strains[keep, pl.ds(first + field - 3, rows, stride=8)] = values * compliance

    def over(first, last, body, width=2):
        def group(index, carry):
            for step in range(width):
                body(EDGE + first + index * width + step)
            return carry

        lax.fori_loop(0, (last - first) // width, group, 0)

    top = EDGE + planes
    move(EDGE - 2, do_yz=False)
    move(top + 1, do_x=False)
    over(-1, planes + 1, move)
    for place in range(EDGE - 3, EDGE):
        strain(place, do_yz=place == EDGE - 1)
    over(0, planes, functools.partial(strain, keep=0))
    for place in range(top, top + 3):
        strain(place, do_yz=place < top + 2)
    slots, points_each = cells.shape
    lane_bits = lanes.bit_length() - 1
    tall = lax.broadcasted_iota(jnp.int32, (8, lanes), 1)

    def sampled(which, slot):
        found = jnp.zeros((8, lanes), f32)
        for point in range(points_each):
            cell = cells[slot, point]
            first = pl.multiple_of((cell >> lane_bits) << 3, 8)
            turned = pltpu.roll(strains[which, pl.ds(first, 8)], (point - cell) & (lanes - 1), 1)
            found = jnp.where(tall == point, turned, found)
        return found

    def move_and_sample(index, carry):
        for step in range(2):
            move(EDGE - 1 + 2 * index + step)
        early[index] = sampled(0, index)
        return carry

    cell_copy.wait()
    move(EDGE - 2, do_yz=False)
    move(top + 1, do_x=False)
    together = min(slots, (planes + 2) // 2)
    lax.fori_loop(0, together, move_and_sample, 0)
    over(2 * together - 1, planes + 1, move)
    for slot in range(together, slots):
        early[slot] = sampled(0, slot)
    out_copies = [
        pltpu.make_async_copy(moving.at[:, slab, inner], velocity_out, out_sems.at[0]),
        pltpu.make_async_copy(pulling.at[:, slab, inner], stress_out, out_sems.at[1]),
    ]
    out_copies[0].start()
    over(0, planes, functools.partial(strain, keep=1))
    out_copies[1].start()

    slip_copy.wait()

    def add_slot(slot, new):
        pair = [
            jnp.concatenate([values[part : part + 1] for part in range(6)], axis=1)
            for values in (early[slot], sampled(1, slot))
        ]
        pair = jnp.concatenate(pair + [jnp.zeros((6, 6 * points_each), f32)], axis=0).astype(bf16)
        return new + lax.dot_general(pair, slips[slot], (((1,), (1,)), ((), ())), preferred_element_type=f32)

    new = lax.fori_loop(0, live[0], add_slot, jnp.zeros((8, slips.shape[1]), f32))
    new = jnp.concatenate([new, jnp.zeros((lanes - 8, slips.shape[1]), f32)], axis=0).T
    column = lax.broadcasted_iota(jnp.int32, new.shape, 1)
    exponent, steps = in_steps(new)
    steps = jnp.where(column == 2, exponent, jnp.where(column == 3, exponents[...], steps))
    tail[...] = steps.astype(jnp.int32).astype(jnp.int16)
    sum_copies[1].start()
    for copy in out_copies + sum_copies:
        copy.wait()


def sum_kernel(sums, out, values, news):
    share, samples = out.shape
    half = samples // 2
    steps = sums[:, half:].astype(jnp.int32).astype(f32)
    news[...] = steps * jnp.exp2(steps[:, 2:3])
    values[...] = sums[:, :half].astype(jnp.int32).astype(f32) * jnp.exp2(steps[:, 3:4])
    halves = [jnp.zeros((share, half), f32) for _ in range(2)]
    new = jnp.zeros((share, news.shape[1]), f32)
    for device in range(sums.shape[0] // share):
        at = slice(device * share, (device + 1) * share)
        halves[device % 2] = halves[device % 2] + values[at]
        new = new + news[at]
    out[...] = jnp.concatenate([jnp.concatenate(halves, axis=1)[:, 2:], new[:, 0:2]], axis=1)


def per_device(
    velocity,
    stress,
    material,
    buoyancy_table,
    lame_table,
    shear_table,
    fault_cells,
    block_count,
    strain_history,
    slip_weights,
):
    count = lax.axis_size("gx")
    planes, rows, lanes = material.shape
    slots, parts, points_each, samples = strain_history.shape
    ruptures = slip_weights.shape[1]
    share = ruptures // count
    whole = pl.BlockSpec(memory_space=pltpu.VMEM)
    scalars = pl.BlockSpec(memory_space=pltpu.SMEM)
    anywhere = pl.BlockSpec(memory_space=pl.ANY)
    params = pltpu.CompilerParams(vmem_limit_bytes=24 * 1024 * 1024)

    def stay(array):
        return pltpu.with_memory_space_constraint(array, pltpu.HBM)

    live = block_count
    velocity, stress, material, slip_weights, cells = [
        stay(array) for array in (velocity, stress, material, slip_weights, fault_cells)
    ]
    tables = [stay(table) for table in (buoyancy_table, lame_table, shear_table)]
    table_scratch = [pltpu.SMEM(table.shape, f32) for table in tables]
    history = stay(strain_history.reshape(slots, parts * points_each, samples))

    def cost(flops, size):
        return pl.CostEstimate(flops=flops, bytes_accessed=size, transcendentals=0)

    halo = pltpu.VMEM((HALO, rows, lanes), bf16)
    extent = planes + 2 * EDGE
    padded = [pltpu.VMEM((fields, extent, rows + 2 * RIM, lanes), f32) for fields in (3, 6)]
    across, within = pl.pallas_call(
        pack_kernel,
        out_shape=(halo, halo),
        in_specs=[anywhere] * 4,
        out_specs=(whole, whole),
        scratch_shapes=[
            *padded,
            pltpu.VMEM(material.shape, jnp.int32),
            table_scratch[0],
            pltpu.SemaphoreType.DMA((4,)),
        ],
        compiler_params=params,
        name="pack_halos",
    )(velocity, stress, material, tables[0])
    chips = [(i, i + 1) for i in range(1, count - 1, 2)]
    cores = [(i, i + 1) for i in range(0, count - 1, 2)]
    cores = cores + [(j, i) for i, j in cores]
    packed = within
    across = lax.ppermute(across, "gx", chips + [(j, i) for i, j in chips])
    within = lax.ppermute(within, "gx", cores)

    half = pltpu.VMEM((ruptures, samples // 2), f32)
    kept, sent = pl.pallas_call(
        history_kernel,
        out_shape=(half, half),
        in_specs=[scalars] + [anywhere] * 3,
        out_specs=(whole, whole),
        scratch_shapes=[
            pltpu.VMEM(slip_weights.shape, bf16),
            pltpu.VMEM(history.shape, bf16),
            pltpu.VMEM((ruptures, samples), f32),
            pltpu.SemaphoreType.DMA((slots,)),
            pltpu.SemaphoreType.DMA((slots,)),
        ],
        compiler_params=params,
        cost_estimate=cost(10**10, 2 * (history.size + slip_weights.size)),
        name="history_product",
    )(live, slip_weights, history, packed)

    received = lax.ppermute(sent, "gx", cores)
    slab = [pltpu.VMEM(array.shape, array.dtype) for array in (velocity, stress, material)]
    partial, exponents, *slab, entries = pl.pallas_call(
        ready_kernel,
        out_shape=(
            pltpu.VMEM((ruptures, samples // 2), jnp.int16),
            pltpu.VMEM((ruptures, lanes), f32),
            *slab,
            pltpu.VMEM((3 * buoyancy_table.shape[0], lanes), f32),
        ),
        in_specs=[whole] * 2 + [anywhere] * 6,
        out_specs=(whole,) * 6,
        scratch_shapes=table_scratch + [pltpu.SemaphoreType.DMA((6,))],
        compiler_params=params,
        cost_estimate=cost(10**6, 1024 * 1024),
        name="ready_slab",
    )(kept, received, velocity, stress, material, *tables)
    velocity_two, stress_two, sums = pl.pallas_call(
        steps_kernel,
        out_shape=(
            jax.ShapeDtypeStruct(velocity.shape, f32),
            jax.ShapeDtypeStruct(stress.shape, f32),
            jax.ShapeDtypeStruct((ruptures, samples // 2 + lanes), jnp.int16),
        ),
        in_specs=[scalars] + [anywhere] * 2 + [whole] * 8,
        out_specs=(anywhere,) * 3,
        scratch_shapes=[
            *padded,
            pltpu.VMEM((3, extent, rows, lanes), f32),
            pltpu.VMEM((2, planes, rows, lanes), f32),
            pltpu.VMEM((2, planes * rows * 8, lanes), f32),
            pltpu.VMEM((slots, 8, lanes), f32),
            pltpu.VMEM(slip_weights.shape, bf16),
            pltpu.SMEM(cells.shape, jnp.int32),
            pltpu.VMEM((ruptures, lanes), jnp.int16),
            pltpu.SemaphoreType.DMA,
            pltpu.SemaphoreType.DMA,
            pltpu.SemaphoreType.DMA((4,)),
        ],
        compiler_params=params,
        cost_estimate=cost(10**10, 30 * 1024 * 1024),
        name="two_steps",
    )(live, cells, slip_weights, *slab, entries, across, within, partial, exponents)
    sums = lax.all_to_all(sums, "gx", 0, 0, tiled=True)
    seismograms = pl.pallas_call(
        sum_kernel,
        out_shape=jax.ShapeDtypeStruct((share, samples), f32),
        in_specs=[whole],
        out_specs=whole,
        scratch_shapes=[pltpu.VMEM((ruptures, samples // 2), f32), pltpu.VMEM((ruptures, lanes), f32)],
        compiler_params=params,
        name="sum_partials",
    )(sums)
    return (velocity_two, stress_two, seismograms)


def solution(mesh):
    in_specs = (
        P(None, ("site", "gx"), None, None),
        P(None, ("site", "gx"), None, None),
        P("gx", None, None),
        P(),
        P(),
        P(),
        P("gx", None),
        P("gx"),
        P(("site", "gx"), None, None, None),
        P("gx", None, None),
    )
    out_specs = (
        P(None, ("site", "gx"), None, None),
        P(None, ("site", "gx"), None, None),
        P(("site", "gx"), None),
    )
    return jax.shard_map(
        per_device, mesh=mesh, in_specs=in_specs, out_specs=out_specs, check_vma=False
    )
```

profile of v0, /device:TPU:0, one launch (start us, length us, event | category | flops | bytes accessed | tf_op | source)
XLA Modules:
  0.0 35.1 jit_solution(14380742481734324497)
XLA Ops:
  0.6 1.7 %pack_halos.1 = (bf16[35,32,128]{2,1,0:T(8,128)(2,1)S(1)}, bf16[35,32,128]{2,1,0:T(8,128)(2,1)S(1)}) custom-call(f32[3,8,32,128]{3,2,1,0:T(8,128)} %velocity_from.3, f32[6,8,32,128]{3,2,1,0:T(8,128)} %stress_from.3, s32[8,32,128]{2,1,0:T(8,128)} %material_from.3, f32[8]{0:T(128)} %buoyancy_from.3), custom_call_target="tpu_custom_call" | custom-call | tf_op jit(solution)/shard_map/pack_halos/pallas_call | solution.py:516
  2.3 0.7 %collective-permute-start.1 = (bf16[35,32,128]{2,1,0:T(8,128)(2,1)S(1)}, bf16[35,32,128]{2,1,0:T(8,128)(2,1)S(1)}, u32[]{:S(2)}, u32[]{:S(2)}) collective-permute-start(bf16[35,32,128]{2,1,0:T(8,128)(2,1)S(1)} %get-tuple-element.23), channel_id=1, source_target_pairs={{1,2},{3,4},{5,6},{7,8},{9,10},{11,12},{13,14},{2,1},{4,3},{6,5},{... | collective-permute-start | bytes 860168 | tf_op jit(solution)/shard_map/ppermute | solution.py:534
  3.0 4.4 %collective-permute-start.2 = (bf16[35,32,128]{2,1,0:T(8,128)(2,1)S(1)}, bf16[35,32,128]{2,1,0:T(8,128)(2,1)S(1)}, u32[]{:S(2)}, u32[]{:S(2)}) collective-permute-start(bf16[35,32,128]{2,1,0:T(8,128)(2,1)S(1)} %get-tuple-element.16.after), channel_id=1, source_target_pairs={{0,1},{2,3},{4,5},{6,7},{8,9},{10,11},{12,13},{14,15},{1,0},{3,2},... | collective-permute-start | bytes 860168 | tf_op jit(solution)/shard_map/ppermute | solution.py:535
  8.1 1.8 %history_product.1 = (f32[256,256]{1,0:T(8,128)S(1)}, f32[256,256]{1,0:T(8,128)S(1)}) custom-call(s32[1]{0:T(128)S(6)} %copy.13.live, bf16[4,256,768]{2,1,0:T(8,128)(2,1)} %weights.3, bf16[4,768,512]{2,1,0:T(8,128)(2,1)} %bitcast.5, bf16[35,32,128]{2,1,0:T(8,128)(2,1)S(1)} %get-tuple-element.16.after), custom_call_target="tpu_custom_call" | custom-call | flops 10000000000 | bytes 4718592 | tf_op jit(solution)/shard_map/history_product/pallas_call | solution.py:538
  9.8 0.1 collective-permute-start
  9.9 1.5 %collective-permute-done.received = f32[256,256]{1,0:T(8,128)S(1)} collective-permute-done((f32[256,256]{1,0:T(8,128)S(1)}, f32[256,256]{1,0:T(8,128)S(1)}, u32[]{:S(2)}, u32[]{:S(2)}) %collective-permute-start) | collective-permute-done | bytes 262176 | tf_op jit(solution)/shard_map/ppermute | solution.py:555
  11.4 1.4 %ready_slab.1 = (s16[256,256]{1,0:T(8,128)(2,1)S(1)}, f32[256,128]{1,0:T(8,128)S(1)}, f32[3,8,32,128]{3,2,1,0:T(8,128)S(1)}, f32[6,8,32,128]{3,2,1,0:T(8,128)S(1...) custom-call(f32[256,256]{1,0:T(8,128)S(1)} %get-tuple-element.17.kept, ...), custom_call_target="tpu_custom_call" | custom-call | flops 1000000 | bytes 1048576 | tf_op jit(solution)/shard_map/ready_slab/pallas_call | solution.py:557
  12.8 0.0 collective-permute-done.1.across
  12.8 0.0 collective-permute-done.2.within
  12.8 5.7 %two_steps.1 = (f32[3,8,32,128]{3,2,1,0:T(8,128)}, f32[6,8,32,128]{3,2,1,0:T(8,128)}, s16[256,384]{1,0:T(8,128)(2,1)S(1)}) custom-call(s32[1]{0:T(128)S(6)} %copy.13.live, s32[4,128]{1,0:T(4,128)} %cells_from.1, bf16[4,256,768]{2,1,0:T(8,128)(2,1)} %weights.3, f32[3,8,32,128]{3,2,1,0:T(8,128)S(1)} %get-tuple-element.19.velocity, ...), custom_call_target="tpu_custom_call" | custom-call | flops 10000000000 | bytes 31457280 | tf_op jit(solution)/shard_map/two_steps/pallas_call | solution.py:572
  18.5 15.7 %all_to_all.11 = s16[16,16,384]{2,1,0:T(8,128)(2,1)S(1)} all-to-all(s16[16,16,384]{2,1,0:T(8,128)(2,1)S(1)} %bitcast.4), channel_id=1, replica_groups=mesh['site'=2,'gx'=16] {'gx'}, dimensions={0} | all-to-all | bytes 393216 | tf_op jit(solution)/shard_map/all_to_all | solution.py:598
  34.2 0.8 %sum_partials.1 = f32[16,512]{1,0:T(8,128)} custom-call(s16[256,384]{1,0:T(8,128)(2,1)S(1)} %bitcast.3), custom_call_target="tpu_custom_call" | custom-call | tf_op jit(solution)/shard_map/sum_partials/pallas_call | solution.py:599
Async XLA Ops:
  2.3 10.5 %collective-permute-start.1 = (bf16[35,32,128]{2,1,0:T(8,128)(2,1)S(1)}, bf16[35,32,128]{2,1,0:T(8,128)(2,1)S(1)}, u32[]{:S(2)}, u32[]{:S(2)}) collective-permute-start(bf16[35,32,128]{2,1,0:T(8,128)(2,1)S(1)} %get-tuple-element.23), channel_id=1, source_target_pairs={{1,2},{3,4},{5,6},{7,8},{9,10},{11,12},{13,14},{2,1},{4,3},{6,5},{... | collective-permute-start | bytes 860168 | tf_op jit(solution)/shard_map/ppermute | solution.py:534
  3.0 9.8 %collective-permute-start.2 = (bf16[35,32,128]{2,1,0:T(8,128)(2,1)S(1)}, bf16[35,32,128]{2,1,0:T(8,128)(2,1)S(1)}, u32[]{:S(2)}, u32[]{:S(2)}) collective-permute-start(bf16[35,32,128]{2,1,0:T(8,128)(2,1)S(1)} %get-tuple-element.16.after), channel_id=1, source_target_pairs={{0,1},{2,3},{4,5},{6,7},{8,9},{10,11},{12,13},{14,15},{1,0},{3,2},... | collective-permute-start | bytes 860168 | tf_op jit(solution)/shard_map/ppermute | solution.py:535
  9.8 1.6 %collective-permute-start = (f32[256,256]{1,0:T(8,128)S(1)}, f32[256,256]{1,0:T(8,128)S(1)}, u32[]{:S(2)}, u32[]{:S(2)}) collective-permute-start(f32[256,256]{1,0:T(8,128)S(1)} %get-tuple-element.18), channel_id=1, source_target_pairs={{0,1},{2,3},{4,5},{6,7},{8,9},{10,11},{12,13},{14,15},{1,0},{3,2},... | collective-permute-start | bytes 786440 | tf_op jit(solution)/shard_map/ppermute | solution.py:555
where the time goes:
time: 35.6 us; the launch traced here: 35.1 us
  blocking collectives  15.7 us (44%)
  Pallas kernels  11.4 us (32%)
  starting transfers between devices  5.13 us (14%)
  waiting for transfers between devices  1.53 us (4%)
  between operations  1.34 us (4%)
    all_to_all x1, blocking collectives, per_device(): sums = lax.all_to_all(sums, 'gx', 0, 0, tiled=True)  15.7 us
    pallas_call x1, Pallas kernels, per_device(): pl.pallas_call(steps_kernel, out_shape=(jax.ShapeDtypeStruct(velocity.sha...  5.7 us
    ppermute x1, starting transfers between devices, per_device(): within = lax.ppermute(within, 'gx', cores)  4.38 us
    pallas_call x1, Pallas kernels, per_device(): pl.pallas_call(history_kernel, out_shape=(half, half), in_specs=[scalars]...  1.77 us
    pallas_call x1, Pallas kernels, per_device(): pl.pallas_call(pack_kernel, out_shape=(halo, halo), in_specs=[anywhere] *...  1.7 us
    ppermute x1, waiting for transfers between devices, per_device(): received = lax.ppermute(sent, 'gx', cores)  1.52 us
    pallas_call x1, Pallas kernels, per_device(): pl.pallas_call(ready_kernel, out_shape=(pltpu.VMEM((ruptures, samples //...  1.35 us
    pallas_call x1, Pallas kernels, per_device(): pl.pallas_call(sum_kernel, out_shape=jax.ShapeDtypeStruct((share, samples...  0.83 us
  transfers between devices with their start and end apart: 3, of which 1 were waited for; matrix products, arithmetic and copies ran while one was open for 0% of the time, Pallas kernels for 9%

commit v1 on v0

--- a/solution.py
+++ b/solution.py
@@ -284,7 +284,7 @@
     factors,
     strain_factors,
     strains,
-    early,
+    pairs,
     slips,
     cells,
     tail,
@@ -416,20 +416,9 @@
             found = jnp.where(tall == point, turned, found)
         return found
 
-    def move_and_sample(index, carry):
-        for step in range(2):
-            move(EDGE - 1 + 2 * index + step)
-        early[index] = sampled(0, index)
-        return carry
-
-    cell_copy.wait()
     move(EDGE - 2, do_yz=False)
     move(top + 1, do_x=False)
-    together = min(slots, (planes + 2) // 2)
-    lax.fori_loop(0, together, move_and_sample, 0)
-    over(2 * together - 1, planes + 1, move)
-    for slot in range(together, slots):
-        early[slot] = sampled(0, slot)
+    over(-1, planes + 1, move)
     out_copies = [
         pltpu.make_async_copy(moving.at[:, slab, inner], velocity_out, out_sems.at[0]),
         pltpu.make_async_copy(pulling.at[:, slab, inner], stress_out, out_sems.at[1]),
@@ -438,17 +427,21 @@
     over(0, planes, functools.partial(strain, keep=1))
     out_copies[1].start()
 
+    pairs[...] = jnp.zeros(pairs.shape, f32)
+    cell_copy.wait()
+
+    def sample_slot(slot, carry):
+        for which in range(2):
+            found = sampled(which, slot)
+            pairs[slot, which : which + 1] = jnp.concatenate([found[part : part + 1] for part in range(6)], axis=1)
+        return carry
+
+    lax.fori_loop(0, live[0], sample_slot, 0)
     slip_copy.wait()
-
-    def add_slot(slot, new):
-        pair = [
-            jnp.concatenate([values[part : part + 1] for part in range(6)], axis=1)
-            for values in (early[slot], sampled(1, slot))
-        ]
-        pair = jnp.concatenate(pair + [jnp.zeros((6, 6 * points_each), f32)], axis=0).astype(bf16)
-        return new + lax.dot_general(pair, slips[slot], (((1,), (1,)), ((), ())), preferred_element_type=f32)
-
-    new = lax.fori_loop(0, live[0], add_slot, jnp.zeros((8, slips.shape[1]), f32))
+    new = jnp.zeros((8, slips.shape[1]), f32)
+    for slot in range(slots):
+        pair = pairs[slot].astype(bf16)
+        new = new + lax.dot_general(pair, slips[slot], (((1,), (1,)), ((), ())), preferred_element_type=f32)
     new = jnp.concatenate([new, jnp.zeros((lanes - 8, slips.shape[1]), f32)], axis=0).T
     column = lax.broadcasted_iota(jnp.int32, new.shape, 1)
     exponent, steps = in_steps(new)
@@ -583,7 +576,7 @@
             pltpu.VMEM((3, extent, rows, lanes), f32),
             pltpu.VMEM((2, planes, rows, lanes), f32),
             pltpu.VMEM((2, planes * rows * 8, lanes), f32),
-            pltpu.VMEM((slots, 8, lanes), f32),
+            pltpu.VMEM((slots, 8, parts * points_each), f32),
             pltpu.VMEM(slip_weights.shape, bf16),
             pltpu.SMEM(cells.shape, jnp.int32),
             pltpu.VMEM((ruptures, lanes), jnp.int16),

time: 35.6 us -> 35.7 us (level)
  blocking collectives: 15.7 us -> 16.5 us
  Pallas kernels: 11.4 us -> 11 us
    all_to_all x1, blocking collectives: 15.7 us -> 16.5 us  [per_device(): sums = lax.all_to_all(sums, 'gx', 0, 0, tiled=True)]
    pallas_call x1, Pallas kernels: 5.7 us -> 5.3 us  [per_device(): pl.pallas_call(steps_kernel, out_shape=(jax.ShapeDtypeStruct(velocity.sha...]
where the time goes in v1:
time: 35.7 us; the launch traced here: 35.4 us
  blocking collectives  16.5 us (46%)
  Pallas kernels  11 us (31%)
  starting transfers between devices  5.13 us (14%)
  waiting for transfers between devices  1.53 us (4%)
  between operations  1.34 us (4%)
    all_to_all x1, blocking collectives, per_device(): sums = lax.all_to_all(sums, 'gx', 0, 0, tiled=True)  16.5 us
    pallas_call x1, Pallas kernels, per_device(): pl.pallas_call(steps_kernel, out_shape=(jax.ShapeDtypeStruct(velocity.sha...  5.3 us
    ppermute x1, starting transfers between devices, per_device(): within = lax.ppermute(within, 'gx', cores)  4.38 us
    pallas_call x1, Pallas kernels, per_device(): pl.pallas_call(history_kernel, out_shape=(half, half), in_specs=[scalars]...  1.77 us
    pallas_call x1, Pallas kernels, per_device(): pl.pallas_call(pack_kernel, out_shape=(halo, halo), in_specs=[anywhere] *...  1.7 us
    ppermute x1, waiting for transfers between devices, per_device(): received = lax.ppermute(sent, 'gx', cores)  1.52 us
    pallas_call x1, Pallas kernels, per_device(): pl.pallas_call(ready_kernel, out_shape=(pltpu.VMEM((ruptures, samples //...  1.35 us
    pallas_call x1, Pallas kernels, per_device(): pl.pallas_call(sum_kernel, out_shape=jax.ShapeDtypeStruct((share, samples...  0.83 us
  transfers between devices with their start and end apart: 3, of which 1 were waited for; matrix products, arithmetic and copies ran while one was open for 0% of the time, Pallas kernels for 9%

profile of v1, /device:TPU:0, one launch (start us, length us, event | category | flops | bytes accessed | tf_op | source)
XLA Modules:
  0.0 35.4 jit_solution(15175651055866275099)
XLA Ops:
  0.6 1.7 %pack_halos.1 = (bf16[35,32,128]{2,1,0:T(8,128)(2,1)S(1)}, bf16[35,32,128]{2,1,0:T(8,128)(2,1)S(1)}) custom-call(f32[3,8,32,128]{3,2,1,0:T(8,128)} %velocity_from.3, f32[6,8,32,128]{3,2,1,0:T(8,128)} %stress_from.3, s32[8,32,128]{2,1,0:T(8,128)} %material_from.3, f32[8]{0:T(128)} %buoyancy_from.3), custom_call_target="tpu_custom_call" | custom-call | tf_op jit(solution)/shard_map/pack_halos/pallas_call | solution.py:509
  2.3 0.7 %collective-permute-start.1 = (bf16[35,32,128]{2,1,0:T(8,128)(2,1)S(1)}, bf16[35,32,128]{2,1,0:T(8,128)(2,1)S(1)}, u32[]{:S(2)}, u32[]{:S(2)}) collective-permute-start(bf16[35,32,128]{2,1,0:T(8,128)(2,1)S(1)} %get-tuple-element.23), channel_id=1, source_target_pairs={{1,2},{3,4},{5,6},{7,8},{9,10},{11,12},{13,14},{2,1},{4,3},{6,5},{... | collective-permute-start | bytes 860168 | tf_op jit(solution)/shard_map/ppermute | solution.py:527
  3.0 4.4 %collective-permute-start.2 = (bf16[35,32,128]{2,1,0:T(8,128)(2,1)S(1)}, bf16[35,32,128]{2,1,0:T(8,128)(2,1)S(1)}, u32[]{:S(2)}, u32[]{:S(2)}) collective-permute-start(bf16[35,32,128]{2,1,0:T(8,128)(2,1)S(1)} %get-tuple-element.16.after), channel_id=1, source_target_pairs={{0,1},{2,3},{4,5},{6,7},{8,9},{10,11},{12,13},{14,15},{1,0},{3,2},... | collective-permute-start | bytes 860168 | tf_op jit(solution)/shard_map/ppermute | solution.py:528
  8.1 1.8 %history_product.1 = (f32[256,256]{1,0:T(8,128)S(1)}, f32[256,256]{1,0:T(8,128)S(1)}) custom-call(s32[1]{0:T(128)S(6)} %copy.13.live, bf16[4,256,768]{2,1,0:T(8,128)(2,1)} %weights.3, bf16[4,768,512]{2,1,0:T(8,128)(2,1)} %bitcast.5, bf16[35,32,128]{2,1,0:T(8,128)(2,1)S(1)} %get-tuple-element.16.after), custom_call_target="tpu_custom_call" | custom-call | flops 10000000000 | bytes 4718592 | tf_op jit(solution)/shard_map/history_product/pallas_call | solution.py:531
  9.8 0.1 collective-permute-start
  9.9 1.5 %collective-permute-done.received = f32[256,256]{1,0:T(8,128)S(1)} collective-permute-done((f32[256,256]{1,0:T(8,128)S(1)}, f32[256,256]{1,0:T(8,128)S(1)}, u32[]{:S(2)}, u32[]{:S(2)}) %collective-permute-start) | collective-permute-done | bytes 262176 | tf_op jit(solution)/shard_map/ppermute | solution.py:548
  11.4 1.4 %ready_slab.1 = (s16[256,256]{1,0:T(8,128)(2,1)S(1)}, f32[256,128]{1,0:T(8,128)S(1)}, f32[3,8,32,128]{3,2,1,0:T(8,128)S(1)}, f32[6,8,32,128]{3,2,1,0:T(8,128)S(1...) custom-call(f32[256,256]{1,0:T(8,128)S(1)} %get-tuple-element.17.kept, ...), custom_call_target="tpu_custom_call" | custom-call | flops 1000000 | bytes 1048576 | tf_op jit(solution)/shard_map/ready_slab/pallas_call | solution.py:550
  12.8 0.0 collective-permute-done.1.across
  12.8 0.0 collective-permute-done.2.within
  12.8 5.3 %two_steps.1 = (f32[3,8,32,128]{3,2,1,0:T(8,128)}, f32[6,8,32,128]{3,2,1,0:T(8,128)}, s16[256,384]{1,0:T(8,128)(2,1)S(1)}) custom-call(s32[1]{0:T(128)S(6)} %copy.13.live, s32[4,128]{1,0:T(4,128)} %cells_from.1, bf16[4,256,768]{2,1,0:T(8,128)(2,1)} %weights.3, f32[3,8,32,128]{3,2,1,0:T(8,128)S(1)} %get-tuple-element.19.velocity, ...), custom_call_target="tpu_custom_call" | custom-call | flops 10000000000 | bytes 31457280 | tf_op jit(solution)/shard_map/two_steps/pallas_call | solution.py:565
  18.1 16.5 %all_to_all.11 = s16[16,16,384]{2,1,0:T(8,128)(2,1)S(1)} all-to-all(s16[16,16,384]{2,1,0:T(8,128)(2,1)S(1)} %bitcast.4), channel_id=1, replica_groups=mesh['site'=2,'gx'=16] {'gx'}, dimensions={0} | all-to-all | bytes 393216 | tf_op jit(solution)/shard_map/all_to_all | solution.py:591
  34.6 0.8 %sum_partials.1 = f32[16,512]{1,0:T(8,128)} custom-call(s16[256,384]{1,0:T(8,128)(2,1)S(1)} %bitcast.3), custom_call_target="tpu_custom_call" | custom-call | tf_op jit(solution)/shard_map/sum_partials/pallas_call | solution.py:592
Async XLA Ops:
  2.3 10.5 %collective-permute-start.1 = (bf16[35,32,128]{2,1,0:T(8,128)(2,1)S(1)}, bf16[35,32,128]{2,1,0:T(8,128)(2,1)S(1)}, u32[]{:S(2)}, u32[]{:S(2)}) collective-permute-start(bf16[35,32,128]{2,1,0:T(8,128)(2,1)S(1)} %get-tuple-element.23), channel_id=1, source_target_pairs={{1,2},{3,4},{5,6},{7,8},{9,10},{11,12},{13,14},{2,1},{4,3},{6,5},{... | collective-permute-start | bytes 860168 | tf_op jit(solution)/shard_map/ppermute | solution.py:527
  3.0 9.8 %collective-permute-start.2 = (bf16[35,32,128]{2,1,0:T(8,128)(2,1)S(1)}, bf16[35,32,128]{2,1,0:T(8,128)(2,1)S(1)}, u32[]{:S(2)}, u32[]{:S(2)}) collective-permute-start(bf16[35,32,128]{2,1,0:T(8,128)(2,1)S(1)} %get-tuple-element.16.after), channel_id=1, source_target_pairs={{0,1},{2,3},{4,5},{6,7},{8,9},{10,11},{12,13},{14,15},{1,0},{3,2},... | collective-permute-start | bytes 860168 | tf_op jit(solution)/shard_map/ppermute | solution.py:528
  9.8 1.6 %collective-permute-start = (f32[256,256]{1,0:T(8,128)S(1)}, f32[256,256]{1,0:T(8,128)S(1)}, u32[]{:S(2)}, u32[]{:S(2)}) collective-permute-start(f32[256,256]{1,0:T(8,128)S(1)} %get-tuple-element.18), channel_id=1, source_target_pairs={{0,1},{2,3},{4,5},{6,7},{8,9},{10,11},{12,13},{14,15},{1,0},{3,2},... | collective-permute-start | bytes 786440 | tf_op jit(solution)/shard_map/ppermute | solution.py:548

commit v2 on v1

--- a/solution.py
+++ b/solution.py
@@ -407,13 +407,16 @@
     lane_bits = lanes.bit_length() - 1
     tall = lax.broadcasted_iota(jnp.int32, (8, lanes), 1)
 
-    def sampled(which, slot):
-        found = jnp.zeros((8, lanes), f32)
+    def sampled(slot):
+        found = [jnp.zeros((8, lanes), f32) for _ in range(2)]
         for point in range(points_each):
             cell = cells[slot, point]
             first = pl.multiple_of((cell >> lane_bits) << 3, 8)
-            turned = pltpu.roll(strains[which, pl.ds(first, 8)], (point - cell) & (lanes - 1), 1)
-            found = jnp.where(tall == point, turned, found)
+            shift = (point - cell) & (lanes - 1)
+            hit = tall == point
+            for which in range(2):
+                turned = pltpu.roll(strains[which, pl.ds(first, 8)], shift, 1)
+                found[which] = jnp.where(hit, turned, found[which])
         return found
 
     move(EDGE - 2, do_yz=False)
@@ -431,8 +434,7 @@
     cell_copy.wait()
 
     def sample_slot(slot, carry):
-        for which in range(2):
-            found = sampled(which, slot)
+        for which, found in enumerate(sampled(slot)):
             pairs[slot, which : which + 1] = jnp.concatenate([found[part : part + 1] for part in range(6)], axis=1)
         return carry
 

time: 35.7 us -> 35.3 us (0.989); the launches traced: 35.4 us -> 34.6 us
  blocking collectives: 16.5 us -> 15.9 us
    all_to_all x1, blocking collectives: 16.5 us -> 15.9 us  [per_device(): sums = lax.all_to_all(sums, 'gx', 0, 0, tiled=True)]
where the time goes in v2:
time: 35.3 us; the launch traced here: 34.6 us
  blocking collectives  15.9 us (45%)
  Pallas kernels  10.8 us (31%)
  starting transfers between devices  5.13 us (15%)
  waiting for transfers between devices  1.53 us (4%)
  between operations  1.34 us (4%)
    all_to_all x1, blocking collectives, per_device(): sums = lax.all_to_all(sums, 'gx', 0, 0, tiled=True)  15.9 us
    pallas_call x1, Pallas kernels, per_device(): pl.pallas_call(steps_kernel, out_shape=(jax.ShapeDtypeStruct(velocity.sha...  5.11 us
    ppermute x1, starting transfers between devices, per_device(): within = lax.ppermute(within, 'gx', cores)  4.38 us
    pallas_call x1, Pallas kernels, per_device(): pl.pallas_call(history_kernel, out_shape=(half, half), in_specs=[scalars]...  1.77 us
    pallas_call x1, Pallas kernels, per_device(): pl.pallas_call(pack_kernel, out_shape=(halo, halo), in_specs=[anywhere] *...  1.7 us
    ppermute x1, waiting for transfers between devices, per_device(): received = lax.ppermute(sent, 'gx', cores)  1.52 us
    pallas_call x1, Pallas kernels, per_device(): pl.pallas_call(ready_kernel, out_shape=(pltpu.VMEM((ruptures, samples //...  1.35 us
    pallas_call x1, Pallas kernels, per_device(): pl.pallas_call(sum_kernel, out_shape=jax.ShapeDtypeStruct((share, samples...  0.83 us
  transfers between devices with their start and end apart: 3, of which 1 were waited for; matrix products, arithmetic and copies ran while one was open for 0% of the time, Pallas kernels for 9%

profile of v2, /device:TPU:0, one launch (start us, length us, event | category | flops | bytes accessed | tf_op | source)
XLA Modules:
  0.0 34.6 jit_solution(13277801815178080358)
XLA Ops:
  0.6 1.7 %pack_halos.1 = (bf16[35,32,128]{2,1,0:T(8,128)(2,1)S(1)}, bf16[35,32,128]{2,1,0:T(8,128)(2,1)S(1)}) custom-call(f32[3,8,32,128]{3,2,1,0:T(8,128)} %velocity_from.3, f32[6,8,32,128]{3,2,1,0:T(8,128)} %stress_from.3, s32[8,32,128]{2,1,0:T(8,128)} %material_from.3, f32[8]{0:T(128)} %buoyancy_from.3), custom_call_target="tpu_custom_call" | custom-call | tf_op jit(solution)/shard_map/pack_halos/pallas_call | solution.py:511
  2.3 0.7 %collective-permute-start.1 = (bf16[35,32,128]{2,1,0:T(8,128)(2,1)S(1)}, bf16[35,32,128]{2,1,0:T(8,128)(2,1)S(1)}, u32[]{:S(2)}, u32[]{:S(2)}) collective-permute-start(bf16[35,32,128]{2,1,0:T(8,128)(2,1)S(1)} %get-tuple-element.23), channel_id=1, source_target_pairs={{1,2},{3,4},{5,6},{7,8},{9,10},{11,12},{13,14},{2,1},{4,3},{6,5},{... | collective-permute-start | bytes 860168 | tf_op jit(solution)/shard_map/ppermute | solution.py:529
  3.0 4.4 %collective-permute-start.2 = (bf16[35,32,128]{2,1,0:T(8,128)(2,1)S(1)}, bf16[35,32,128]{2,1,0:T(8,128)(2,1)S(1)}, u32[]{:S(2)}, u32[]{:S(2)}) collective-permute-start(bf16[35,32,128]{2,1,0:T(8,128)(2,1)S(1)} %get-tuple-element.16.after), channel_id=1, source_target_pairs={{0,1},{2,3},{4,5},{6,7},{8,9},{10,11},{12,13},{14,15},{1,0},{3,2},... | collective-permute-start | bytes 860168 | tf_op jit(solution)/shard_map/ppermute | solution.py:530
  8.1 1.8 %history_product.1 = (f32[256,256]{1,0:T(8,128)S(1)}, f32[256,256]{1,0:T(8,128)S(1)}) custom-call(s32[1]{0:T(128)S(6)} %copy.13.live, bf16[4,256,768]{2,1,0:T(8,128)(2,1)} %weights.3, bf16[4,768,512]{2,1,0:T(8,128)(2,1)} %bitcast.5, bf16[35,32,128]{2,1,0:T(8,128)(2,1)S(1)} %get-tuple-element.16.after), custom_call_target="tpu_custom_call" | custom-call | flops 10000000000 | bytes 4718592 | tf_op jit(solution)/shard_map/history_product/pallas_call | solution.py:533
  9.8 0.1 collective-permute-start
  9.9 1.5 %collective-permute-done.received = f32[256,256]{1,0:T(8,128)S(1)} collective-permute-done((f32[256,256]{1,0:T(8,128)S(1)}, f32[256,256]{1,0:T(8,128)S(1)}, u32[]{:S(2)}, u32[]{:S(2)}) %collective-permute-start) | collective-permute-done | bytes 262176 | tf_op jit(solution)/shard_map/ppermute | solution.py:550
  11.4 1.4 %ready_slab.1 = (s16[256,256]{1,0:T(8,128)(2,1)S(1)}, f32[256,128]{1,0:T(8,128)S(1)}, f32[3,8,32,128]{3,2,1,0:T(8,128)S(1)}, f32[6,8,32,128]{3,2,1,0:T(8,128)S(1...) custom-call(f32[256,256]{1,0:T(8,128)S(1)} %get-tuple-element.17.kept, ...), custom_call_target="tpu_custom_call" | custom-call | flops 1000000 | bytes 1048576 | tf_op jit(solution)/shard_map/ready_slab/pallas_call | solution.py:552
  12.8 0.0 collective-permute-done.1.across
  12.8 0.0 collective-permute-done.2.within
  12.8 5.1 %two_steps.1 = (f32[3,8,32,128]{3,2,1,0:T(8,128)}, f32[6,8,32,128]{3,2,1,0:T(8,128)}, s16[256,384]{1,0:T(8,128)(2,1)S(1)}) custom-call(s32[1]{0:T(128)S(6)} %copy.13.live, s32[4,128]{1,0:T(4,128)} %cells_from.1, bf16[4,256,768]{2,1,0:T(8,128)(2,1)} %weights.3, f32[3,8,32,128]{3,2,1,0:T(8,128)S(1)} %get-tuple-element.19.velocity, ...), custom_call_target="tpu_custom_call" | custom-call | flops 10000000000 | bytes 31457280 | tf_op jit(solution)/shard_map/two_steps/pallas_call | solution.py:567
  17.9 15.9 %all_to_all.11 = s16[16,16,384]{2,1,0:T(8,128)(2,1)S(1)} all-to-all(s16[16,16,384]{2,1,0:T(8,128)(2,1)S(1)} %bitcast.4), channel_id=1, replica_groups=mesh['site'=2,'gx'=16] {'gx'}, dimensions={0} | all-to-all | bytes 393216 | tf_op jit(solution)/shard_map/all_to_all | solution.py:593
  33.8 0.8 %sum_partials.1 = f32[16,512]{1,0:T(8,128)} custom-call(s16[256,384]{1,0:T(8,128)(2,1)S(1)} %bitcast.3), custom_call_target="tpu_custom_call" | custom-call | tf_op jit(solution)/shard_map/sum_partials/pallas_call | solution.py:594
Async XLA Ops:
  2.3 10.5 %collective-permute-start.1 = (bf16[35,32,128]{2,1,0:T(8,128)(2,1)S(1)}, bf16[35,32,128]{2,1,0:T(8,128)(2,1)S(1)}, u32[]{:S(2)}, u32[]{:S(2)}) collective-permute-start(bf16[35,32,128]{2,1,0:T(8,128)(2,1)S(1)} %get-tuple-element.23), channel_id=1, source_target_pairs={{1,2},{3,4},{5,6},{7,8},{9,10},{11,12},{13,14},{2,1},{4,3},{6,5},{... | collective-permute-start | bytes 860168 | tf_op jit(solution)/shard_map/ppermute | solution.py:529
  3.0 9.8 %collective-permute-start.2 = (bf16[35,32,128]{2,1,0:T(8,128)(2,1)S(1)}, bf16[35,32,128]{2,1,0:T(8,128)(2,1)S(1)}, u32[]{:S(2)}, u32[]{:S(2)}) collective-permute-start(bf16[35,32,128]{2,1,0:T(8,128)(2,1)S(1)} %get-tuple-element.16.after), channel_id=1, source_target_pairs={{0,1},{2,3},{4,5},{6,7},{8,9},{10,11},{12,13},{14,15},{1,0},{3,2},... | collective-permute-start | bytes 860168 | tf_op jit(solution)/shard_map/ppermute | solution.py:530
  9.8 1.6 %collective-permute-start = (f32[256,256]{1,0:T(8,128)S(1)}, f32[256,256]{1,0:T(8,128)S(1)}, u32[]{:S(2)}, u32[]{:S(2)}) collective-permute-start(f32[256,256]{1,0:T(8,128)S(1)} %get-tuple-element.18), channel_id=1, source_target_pairs={{0,1},{2,3},{4,5},{6,7},{8,9},{10,11},{12,13},{14,15},{1,0},{3,2},... | collective-permute-start | bytes 786440 | tf_op jit(solution)/shard_map/ppermute | solution.py:550
